TPU v7x, 256 devices: a whole 4x4x8 slice. The times are simulated.
256 devices in a mesh: space: 64 (over x, z, core), rep: 4 (over y).
Axes of the slice: x: 4, y: 4, z: 8, core: 2. Of those that a mesh axis runs over, the one named last changes fastest.
Arguments:
- voxel_feats: bfloat16 [4, 96, 98304], P('rep', None, 'space'), may hold values from -6 to 6
- kernel_map: int32 [4, 27, 98304], P('rep', None, 'space'), may hold values from 0 to 2304, as said below
- halo_down: int32 [4, 24576], P('rep', 'space'), may hold values from 0 to 1535
- halo_up: int32 [4, 24576], P('rep', 'space'), may hold values from 0 to 1535
- route_slot: int32 [4, 98304], P('rep', 'space'), may hold values from 0 to 1535, as said below
- recv_target: int32 [4, 98304], P('rep', 'space'), may hold values from 0 to 6143, as said below
- subm_weight: bfloat16 [27, 96, 96], replicated, may hold values from -0.125 to 0.125
- down_weight: bfloat16 [8, 96, 192], replicated, may hold values from -0.21875 to 0.21875
- coarse_grad: bfloat16 [4, 192, 49152], P('rep', None, 'space'), may hold values from -0.0134887695 to 0.0134887695
Outputs:
- coarse_feats: bfloat16 [4, 192, 49152], P('rep', None, 'space')
- subm_grad: float32 [27, 96, 96], replicated
- down_grad: float32 [8, 96, 192], replicated
Inputs may be any that keep to these rules, and one draw needn't show every extreme that they name: `kernel_map`: row 27 // 2 (the centre) of a device's block names the voxel itself. Other entries: below 1536 a voxel of the same device; 1536 to 1919 the rows received from the lower neighbour in space, in the order of its halo_up list; the next 384 those from the upper neighbour in the order of its halo_down list; 2304 an absent neighbour. `route_slot`: distinct within a device's block: each device sends exactly 24 rows to every new owner, so every slot is used. `recv_target`: distinct within a device's block; entry s * 24 + j belongs to the row that slot j of device s brings.
All inputs are finite; a program needn't handle non-finite values.
Results may differ from a plain program's by a relative error of at most 0.0053.
Values may be sent and summed in bfloat16 or wider, within the bound.
A program may use at most 128 MiB of HBM per device.

v0:
```python
import jax
import jax.numpy as jnp
from jax import lax
from jax.experimental import pallas as pl
from jax.experimental.pallas import tpu as pltpu
from jax.sharding import PartitionSpec as P

C = 96
C2 = 192
OFFSETS = 27
CHILDREN = 8
VOX = 1536
HALO = 384
COARSE = 768
CAP = 24
N_SPACE = 64
N_REP = 4
L = 128
PAD = 32
OWN_SUB = 768
RIM_SUB = 256
QUADS = 7
CHUNK = 256
STEP = 384
SEND_STEP = 192
EARLY = 2
PEERS_AT_ONCE = 8
MIB = 2**20
MESH = pl.DeviceIdType.MESH
BF = jnp.bfloat16
F32 = jnp.float32

SUBM_TILES = 21
DOWN_TILES = 6
SUBM_SHARE = 64
DOWN_SHARE = 48


def lane_iota(rows):
    return lax.broadcasted_iota(jnp.int32, (rows, L), 1).astype(F32).astype(BF)


def split_index(index):
    top = jnp.floor(index * (1.0 / L))
    return top.astype(BF), (index - L * top).astype(BF)


def onehot(top, low, iota, tiles):
    rows = iota.shape[0]
    zero = jnp.zeros((), BF)
    hit = jnp.where(jnp.broadcast_to(low, (rows, L)) == iota, jnp.ones((), BF), zero)
    tops = jnp.broadcast_to(top, (rows, L))
    return jnp.concatenate(
        [jnp.where(tops == jnp.asarray(t, BF), hit, zero) for t in range(tiles)], axis=1
    )


def onehot_of_row(row, rows):
    spread = jnp.broadcast_to(row, (rows, row.shape[1])).astype(BF)
    iota = lax.broadcasted_iota(jnp.int32, spread.shape, 0).astype(F32).astype(BF)
    return jnp.where(spread == iota, jnp.ones((), BF), jnp.zeros((), BF))


def padded_rows(x, rows):
    return jnp.concatenate([x, jnp.zeros((rows - x.shape[0], x.shape[1]), x.dtype)], axis=0)


def dot(a, b):
    return jnp.dot(a, b, preferred_element_type=F32)


def aligned(i, n):
    return pl.ds(pl.multiple_of(i * n, n), n)


def pack(blocks):
    piece = lambda k, lo, hi: blocks[:, k * L + lo:k * L + hi]
    return [
        jnp.concatenate([piece(0, 0, C), piece(1, 0, 32)], axis=1),
        jnp.concatenate([piece(1, 32, C), piece(2, 0, 64)], axis=1),
        jnp.concatenate([piece(2, 64, C), piece(3, 0, C)], axis=1),
    ]


def tiles_of_block(k):
    q, r = divmod(k, 4)
    pieces = []
    if r:
        pieces.append((3 * q + r - 1, L - 32 * r, L))
    if r < 3:
        pieces.append((3 * q + r, 0, C - 32 * r))
    return pieces


class Place:
    def __init__(self):
        space, y = lax.axis_index("space"), lax.axis_index("rep")
        core, z, x = space % 2, (space // 2) % 8, space // 16
        at = lambda xx, zz, cc: (xx * 8 + zz) * 2 + cc
        self.space, self.rep, self.core, self.z = space, y, core, z
        self.partner = (at(x, z, 1 - core), y)
        self.plane = [(at((x + d // 4) % 4, z, core), (y + d % 4) % 4) for d in range(16)]
        self.plane_to = [((x + d // 4) % 4) * 4 + (y + d % 4) % 4 for d in range(16)]
        self.plane_from = [((x + 4 - d // 4) % 4) * 4 + (y + 4 - d % 4) % 4 for d in range(16)]
        self.column = [(at(x, (z + d) % 8, core), y) for d in range(8)]
        self.column_from = [(z + 8 - d) % 8 for d in range(8)]


def remote(src, dst, sems, i, peer):
    return pltpu.make_async_remote_copy(
        src_ref=src, dst_ref=dst, send_sem=sems.at[0, i], recv_sem=sems.at[1, i],
        device_id=peer, device_id_type=MESH,
    )


class Reducer:
    @staticmethod
    def scratch(share):
        return [
            pltpu.VMEM((32 * share, L), F32),
            pltpu.VMEM((16 * share, L), BF),
            pltpu.VMEM((16 * share, L), BF),
            pltpu.VMEM((16, share, L), BF),
            pltpu.VMEM((16, share, L), BF),
            pltpu.VMEM((share, L), BF),
            pltpu.VMEM((8, share, L), BF),
            pltpu.VMEM((32 * share, L), BF),
            pltpu.SemaphoreType.DMA((2, 16)),
            pltpu.SemaphoreType.DMA((2, 16)),
            pltpu.SemaphoreType.DMA((2, 8)),
            pltpu.SemaphoreType.DMA((2, 16)),
            pltpu.SemaphoreType.DMA((2, 16)),
        ]

    def __init__(self, place, share, refs):
        self.place, self.share = place, share
        (self.mine, self.theirs, self.pair, self.psend, self.plane, self.zsend, self.column, self.full,
         self.pair_sems, self.plane_sems, self.z_sems, self.back_sems, self.over_sems) = refs
        self.sends = []

    def go(self, copy):
        copy.start()
        self.sends.append(copy)
        return copy

    def start_pair(self):
        p, n = self.place, self.share
        self.theirs[...] = self.mine[aligned(1 - p.core, 16 * n)].astype(BF)
        self.in_pair = []
        for d in range(16):
            at = aligned(p.plane_to[d], n)
            self.in_pair.append(self.go(
                remote(self.theirs.at[at], self.pair.at[at], self.pair_sems, d, p.partner)))

    def start_plane(self):
        p, n = self.place, self.share
        self.in_plane = []
        for d in list(range(1, 16)) + [0]:
            self.in_pair[d].wait_recv()
            both = (self.mine[aligned(p.core * 16 + p.plane_to[d], n)]
                    + self.pair[aligned(p.plane_to[d], n)].astype(F32))
            if d:
                self.psend[d] = both.astype(BF)
                self.in_plane.append(self.go(
                    remote(self.psend.at[d], self.plane.at[d], self.plane_sems, d, p.plane[d])))
        self.total = both

    def start_column(self):
        p = self.place
        total = self.total
        for d in range(1, 16):
            self.in_plane[d - 1].wait_recv()
            total += self.plane[d].astype(F32)
        self.zsend[...] = total.astype(BF)
        self.in_column = []
        for d in range(1, 8):
            self.in_column.append(self.go(
                remote(self.zsend, self.column.at[p.z], self.z_sems, d, p.column[d])))
        self.column[p.z] = total.astype(BF)

    def start_back(self):
        p, n = self.place, self.share
        for copy in self.in_column:
            copy.wait_recv()
        total = self.column[0].astype(F32)
        for z in range(1, 8):
            total += self.column[z].astype(F32)
        here = aligned(p.core * 16 + p.plane_to[0], n)
        self.full[here] = total.astype(BF)
        self.in_back = []
        for d in range(1, 16):
            self.in_back.append(self.go(
                remote(self.full.at[here], self.full.at[here], self.back_sems, d, p.plane[d])))

    def start_over(self):
        p, n = self.place, self.share
        self.in_over = []
        for d in range(16):
            if d:
                self.in_back[d - 1].wait_recv()
            at = aligned(p.core * 16 + p.plane_from[d], n)
            self.in_over.append(self.go(
                remote(self.full.at[at], self.full.at[at], self.over_sems, d, p.partner)))

    def finish(self):
        for copy in self.in_over:
            copy.wait_recv()

    def drain(self):
        for copy in self.sends:
            copy.wait_send()


def swap_copy(src, dst, send_sem, recv_sem, peer, me, rep):
    return pltpu.make_async_remote_copy(
        src_ref=src.at[peer], dst_ref=dst.at[me], send_sem=send_sem, recv_sem=recv_sem,
        device_id=(peer, rep), device_id_type=MESH,
    )


def wait_swapped(src, dst, send_sem, recv_sem, me, rep, sent):
    others = pl.ds(0, N_SPACE - 1)
    copies = pltpu.make_async_remote_copy(
        src_ref=src.at[others], dst_ref=dst.at[others], send_sem=send_sem, recv_sem=recv_sem,
        device_id=((me + 1) % N_SPACE, rep), device_id_type=MESH,
    )
    if sent:
        copies.wait_send()
    else:
        copies.wait_recv()


def rows_of_group(ref, group):
    return jnp.concatenate(
        [ref[group * PEERS_AT_ONCE + i].astype(F32)[:CAP] for i in range(PEERS_AT_ONCE)], axis=0
    )


def step_kernel(
    feats_ref, kmap_ref, up_ref, down_ref, route_ref, target_ref, w_ref, wd_ref, cg_ref,
    coarse_ref, subm_ref, dsum_ref,
    ordered, own, table, rim, which_buf, wpad, wdpad, gath, pre_buf, pre_grads, cgt, back, cells_in,
    hsend, hrecv, bsend, brecv, fsend, frecv, halo_sems, swap_sems, *reduce_refs,
):
    place = Place()
    me, rep = place.space, place.rep
    above, below = (me + 1) % N_SPACE, (me + N_SPACE - 1) % N_SPACE
    barrier = pltpu.get_barrier_semaphore()

    @pl.loop(1, N_SPACE)
    def _(d):
        pl.semaphore_signal(barrier, inc=1, device_id=((me + d) % N_SPACE, rep), device_id_type=MESH)

    others = [place.plane[d] for d in range(16) if d % 4]
    for peer in others:
        pl.semaphore_signal(barrier, inc=1, device_id=peer, device_id_type=MESH)

    own[...] = padded_rows(feats_ref[0].astype(F32), L).T.astype(BF)
    halo_rows = jnp.concatenate([up_ref[...], down_ref[...]], axis=1).astype(F32)
    halo_cols = jnp.broadcast_to(halo_rows, (8, 2 * HALO)).T
    iota_h = lane_iota(HALO)
    for side in range(2):
        top, low = split_index(halo_cols[side * HALO:(side + 1) * HALO, :1])
        hsend[side] = dot(onehot(top, low, iota_h, VOX // L), own[...]).astype(BF)

    target = target_ref[...].astype(F32)
    child = jnp.floor((target + 0.5) * (1.0 / COARSE))
    cell = target - COARSE * child
    wdpad[...] = jnp.zeros_like(wdpad)
    for k in range(CHILDREN):
        wdpad[k * L:k * L + C, :C2] = wd_ref[k]
    for block in range(VOX // CHUNK):
        span = slice(block * CHUNK, (block + 1) * CHUNK)
        hits = jnp.concatenate(
            [onehot_of_row(cell[:, span] - b * CHUNK, CHUNK) for b in range(COARSE // CHUNK)], axis=0
        )
        picked = dot(cg_ref[0], hits).astype(BF)
        cgt[:, span] = picked
        every = dot(wdpad[:, :C2], picked)
        chosen = jnp.zeros((L, CHUNK), F32)
        for k in range(CHILDREN):
            chosen = jnp.where(child[:, span] == k, every[k * L:(k + 1) * L], chosen)
        back[span, :] = chosen.T
    for peer in range(N_SPACE):
        bsend[peer] = padded_rows(back[peer * CAP:(peer + 1) * CAP], PAD).astype(BF)
    brecv[me] = bsend[me]

    neighbours = jnp.concatenate([kmap_ref[k] for k in range(OFFSETS)], axis=0).astype(F32)
    tile = jnp.floor(neighbours * (1.0 / L))
    parts = [padded_rows(x, PAD) for x in (tile, neighbours - L * tile)]
    ordered[:, :L] = padded_rows(jnp.concatenate(parts, axis=0), L).T.astype(BF)
    ordered[:, L:] = own[...]
    for j in range(2):
        table[:, j * L:(j + 1) * L] = own[j * OWN_SUB:(j + 1) * OWN_SUB]
    wpad[...] = jnp.zeros_like(wpad)
    for k in range(OFFSETS):
        wpad[k * L:k * L + C, :C] = w_ref[k]
    route = route_ref[...].astype(F32)
    iota_s = lane_iota(STEP)
    own_tiles = OWN_SUB // L

    def gather_own(turn):
        here = aligned(turn, STEP)
        start = (turn * STEP).astype(F32)
        hits = jnp.concatenate(
            [onehot_of_row(route - (start + off), STEP // 2) for off in (0.0, STEP / 2.0)], axis=0
        )
        mine = dot(hits, ordered[...])
        which = mine[:, :L]
        which_buf[here, :] = which
        pre_buf[here, :] = mine[:, L:]
        second = jnp.where(which >= own_tiles, 1.0, 0.0)
        top, low = (which - own_tiles * second).astype(BF), which.astype(BF)
        for k in range(OFFSETS):
            hot = onehot(top[:, k:k + 1], low[:, PAD + k:PAD + k + 1], iota_s, own_tiles)
            both = dot(hot, table[...])
            picked = jnp.where(second[:, k:k + 1] > 0.5, both[:, L:], both[:, :L])
            gath[here, k * L:(k + 1) * L] = picked.astype(BF)

    pl.loop(0, EARLY)(gather_own)

    to_upper = remote(hsend.at[0], hrecv.at[0], halo_sems, 0, (above, rep))
    to_lower = remote(hsend.at[1], hrecv.at[1], halo_sems, 1, (below, rep))
    pl.semaphore_wait(barrier, N_SPACE - 1 + len(others))
    to_upper.start()
    to_lower.start()

    @pl.loop(1, N_SPACE)
    def _(d):
        swap_copy(bsend, brecv, swap_sems.at[0], swap_sems.at[1], (me + d) % N_SPACE, me, rep).start()

    pl.loop(EARLY, VOX // STEP)(gather_own)

    to_upper.wait()
    to_lower.wait()
    lower = jnp.where(me > 0, hrecv[0], jnp.zeros((), BF))
    upper = jnp.where(me < N_SPACE - 1, hrecv[1], jnp.zeros((), BF))
    rim[:, :L] = lower[:RIM_SUB]
    rim[:HALO - RIM_SUB, L:2 * L] = lower[RIM_SUB:]
    rim[HALO - RIM_SUB:, L:2 * L] = upper[:2 * RIM_SUB - HALO]
    rim[:, 2 * L:] = upper[2 * RIM_SUB - HALO:]

    iota_r = lane_iota(SEND_STEP)
    peers = SEND_STEP // CAP
    rim_tiles = RIM_SUB // L

    @pl.loop(0, VOX // SEND_STEP)
    def _(i):
        turn = (me // peers + i) % (VOX // SEND_STEP)
        here = aligned(turn, SEND_STEP)
        which = which_buf[here, :]
        beyond = which - VOX // L
        kind = jnp.floor(beyond * (1.0 / rim_tiles))
        top, low = (beyond - rim_tiles * kind).astype(BF), which.astype(BF)
        for k in range(OFFSETS):
            lanes = slice(k * L, (k + 1) * L)
            hot = onehot(top[:, k:k + 1], low[:, PAD + k:PAD + k + 1], iota_r, rim_tiles)
            every = dot(hot, rim[...])
            kinds = jnp.broadcast_to(kind[:, k:k + 1], (SEND_STEP, L))
            picked = gath[here, lanes].astype(F32)
            for j in range(3):
                picked = jnp.where(kinds == j, every[:, j * L:(j + 1) * L], picked)
            gath[here, lanes] = picked.astype(BF)
        pre = pre_buf[here, :] + dot(gath[here, :OFFSETS * L], wpad[...])
        pre_buf[here, :] = pre
        fine = pre * jax.nn.sigmoid(pre)
        for j in range(peers):
            peer = turn * peers + j
            fsend[peer] = padded_rows(fine[j * CAP:(j + 1) * CAP], PAD).astype(BF)

            @pl.when(peer != me)
            def _():
                swap_copy(fsend, frecv, swap_sems.at[2], swap_sems.at[3], peer, me, rep).start()

    frecv[me] = fsend[me]

    half = len(reduce_refs) // 2
    subm = Reducer(place, SUBM_SHARE, reduce_refs[:half])
    down = Reducer(place, DOWN_SHARE, reduce_refs[half:])
    groups = N_SPACE // PEERS_AT_ONCE
    group_rows = PEERS_AT_ONCE * CAP
    wait_swapped(bsend, brecv, swap_sems.at[0], swap_sems.at[1], me, rep, False)
    for step in range(VOX // STEP):
        span = slice(step * STEP, (step + 1) * STEP)
        fine_grad = jnp.concatenate([rows_of_group(brecv, 2 * step + i) for i in range(2)], axis=0)
        pre = pre_buf[span, :]
        sig = jax.nn.sigmoid(pre)
        pre_grad = fine_grad * sig * (1.0 + pre * (1.0 - sig))
        pre_grads[:, span] = pre_grad.T.astype(BF)
    gath[:, OFFSETS * L:] = jnp.zeros((VOX, L), BF)
    for quad in range(QUADS):
        grads = dot(pre_grads[...], gath[:, quad * 4 * L:(quad + 1) * 4 * L])[:C]
        for i, packed in enumerate(pack(grads)):
            subm.mine[(3 * quad + i) * C:(3 * quad + i + 1) * C] = packed
    subm.mine[SUBM_TILES * C:] = jnp.zeros((32 * SUBM_SHARE - SUBM_TILES * C, L), F32)
    subm.start_pair()
    subm.start_plane()

    wait_swapped(fsend, frecv, swap_sems.at[2], swap_sems.at[3], me, rep, False)
    child_cols = jnp.broadcast_to(child, (8, VOX)).T
    for group in range(groups):
        span = slice(group * group_rows, (group + 1) * group_rows)
        received = rows_of_group(frecv, group)
        kind = jnp.broadcast_to(child_cols[span, :1], (group_rows, L))
        for k in range(CHILDREN):
            cells_in[span, k * L:(k + 1) * L] = jnp.where(kind == k, received, 0.0).astype(BF)
    for quad in range(CHILDREN // 4):
        grads = dot(cgt[...], cells_in[:, quad * 4 * L:(quad + 1) * 4 * L])
        for i, packed in enumerate(pack(grads)):
            down.mine[(3 * quad + i) * C2:(3 * quad + i + 1) * C2] = packed
    down.mine[DOWN_TILES * C2:] = jnp.zeros((32 * DOWN_SHARE - DOWN_TILES * C2, L), F32)
    down.start_pair()
    subm.start_column()
    down.start_plane()

    def coarse_block(block):
        hits = onehot_of_row(cell - block * CHUNK, CHUNK)
        cells = dot(hits, cells_in[...]).astype(BF)
        coarse_ref[0, :, block * CHUNK:(block + 1) * CHUNK] = dot(cells, wdpad[...]).T[:C2].astype(BF)

    coarse_block(0)
    subm.start_back()
    down.start_column()
    coarse_block(1)
    subm.start_over()
    down.start_back()
    coarse_block(2)
    down.start_over()
    subm.finish()

    subm_ref[...] = subm.full[...]
    down.finish()
    dsum_ref[...] = down.full[...]
    wait_swapped(bsend, brecv, swap_sems.at[0], swap_sems.at[1], me, rep, True)
    wait_swapped(fsend, frecv, swap_sems.at[2], swap_sems.at[3], me, rep, True)
    subm.drain()
    down.drain()


def unpack_kernel(coarse_in, subm_ref, down_ref, coarse_ref, sgrad_ref, dgrad_ref):
    def unpack(full, rows, k):
        parts = [full[t * rows:(t + 1) * rows, lo:hi].astype(F32) for t, lo, hi in tiles_of_block(k)]
        parts.append(jnp.zeros((rows, L - C), F32))
        return jnp.concatenate(parts, axis=1)

    coarse_ref[...] = coarse_in[...]
    for k in range(OFFSETS):
        sgrad_ref[k] = padded_rows(unpack(subm_ref, C, k), L).T[:C, :C]
    for k in range(CHILDREN):
        dgrad_ref[k] = padded_rows(unpack(down_ref, C2, k), 2 * L).T[:C, :C2]


def per_device(
    voxel_feats, kernel_map, halo_down, halo_up, route_slot, recv_target,
    subm_weight, down_weight, coarse_grad,
):
    vmem = pl.BlockSpec(memory_space=pltpu.VMEM)
    swap = pltpu.VMEM((N_SPACE, PAD, L), BF)
    parts = pl.pallas_call(
        step_kernel,
        out_shape=(
            jax.ShapeDtypeStruct((1, C2, COARSE), BF),
            jax.ShapeDtypeStruct((32 * SUBM_SHARE, L), BF),
            jax.ShapeDtypeStruct((32 * DOWN_SHARE, L), BF),
        ),
        in_specs=[vmem] * 9,
        out_specs=(vmem,) * 3,
        scratch_shapes=[
            pltpu.VMEM((VOX, 2 * L), BF),
            pltpu.VMEM((VOX, L), BF),
            pltpu.VMEM((OWN_SUB, 2 * L), BF),
            pltpu.VMEM((RIM_SUB, 3 * L), BF),
            pltpu.VMEM((VOX, L), F32),
            pltpu.VMEM((OFFSETS * L, L), BF),
            pltpu.VMEM((CHILDREN * L, 2 * L), BF),
            pltpu.VMEM((VOX, QUADS * 4 * L), BF),
            pltpu.VMEM((VOX, L), F32),
            pltpu.VMEM((L, VOX), BF),
            pltpu.VMEM((C2, VOX), BF),
            pltpu.VMEM((VOX, L), F32),
            pltpu.VMEM((VOX, CHILDREN * L), BF),
            pltpu.VMEM((2, HALO, L), BF),
            pltpu.VMEM((2, HALO, L), BF),
            swap, swap, swap, swap,
            pltpu.SemaphoreType.DMA((2, 2)),
            pltpu.SemaphoreType.DMA((4,)),
            *Reducer.scratch(SUBM_SHARE),
            *Reducer.scratch(DOWN_SHARE),
        ],
        compiler_params=pltpu.CompilerParams(
            collective_id=0, has_side_effects=True, vmem_limit_bytes=56 * MIB
        ),
        name="step",
    )(
        voxel_feats, kernel_map.transpose(1, 0, 2), halo_up, halo_down, route_slot, recv_target,
        subm_weight, down_weight, coarse_grad,
    )
    return pl.pallas_call(
        unpack_kernel,
        out_shape=(
            jax.ShapeDtypeStruct((1, C2, COARSE), BF),
            jax.ShapeDtypeStruct((OFFSETS, C, C), F32),
            jax.ShapeDtypeStruct((CHILDREN, C, C2), F32),
        ),
        in_specs=[vmem] * 3,
        out_specs=(vmem,) * 3,
        name="unpack",
    )(*parts)


def solution(mesh):
    in_specs = (
        P("rep", None, "space"),
        P("rep", None, "space"),
        P("rep", "space"),
        P("rep", "space"),
        P("rep", "space"),
        P("rep", "space"),
        P(),
        P(),
        P("rep", None, "space"),
    )
    out_specs = (P("rep", None, "space"), P(), P())
    return jax.shard_map(
        per_device, mesh=mesh, in_specs=in_specs, out_specs=out_specs, check_vma=False
    )
```

profile of v0, /device:TPU:1, one launch (start us, length us, event | category | flops | bytes accessed | tf_op | source)
XLA Modules:
  0.0 88.8 jit_solution(13082912734904378394)
XLA Ops:
  0.6 84.7 %step.1 = (bf16[1,192,768]{2,1,0:T(8,128)(2,1)}, bf16[2048,128]{1,0:T(8,128)(2,1)}, bf16[1536,128]{1,0:T(8,128)(2,1)}) custom-call(bf16[1,96,1536]{2,1,0:T(8,128)(2,1)} %feats_ref.1, s32[27,1,1536]{2,1,0:T(1,128)} %bitcast.1, s32[1,384]{1,0:T(1,128)} %up_ref.1, s32[1,384]{1,0:T(1,128)} %down_ref.1, s32[1,1536]{1,0:T(1,128)} %route_ref.1, ...), custom_call_target="tpu_custom_call" | custom-call | tf_op jit(solution)/shard_map/step/pallas_call | solution.py:459
  85.4 3.4 %unpack.1 = (bf16[1,192,768]{2,1,0:T(8,128)(2,1)}, f32[27,96,96]{2,1,0:T(8,128)}, f32[8,96,192]{2,1,0:T(8,128)}) custom-call(bf16[1,192,768]{2,1,0:T(8,128)(2,1)} %get-tuple-element.6.coarse_in, bf16[2048,128]{1,0:T(8,128)(2,1)} %get-tuple-element.7.subm_ref, bf16[1536,128]{1,0:T(8,128)(2,1)} %get-tuple-element.8.down_ref), custom_call_target="tpu_custom_call" | custom-call | tf_op jit(solution)/shard_map/unpack/pallas_call | solution.py:498
where the time goes:
time: 88.9 us; the launch traced here: 88.8 us
  Pallas kernels  88.1 us (99%)
    pallas_call x1, Pallas kernels, per_device(): pl.pallas_call(step_kernel, out_shape=(jax.ShapeDtypeStruct((1, C2, COARS...  84.7 us
    pallas_call x1, Pallas kernels, per_device(): pl.pallas_call(unpack_kernel, out_shape=(jax.ShapeDtypeStruct((1, C2, COA...  3.36 us

commit v1 on v0

--- a/solution.py
+++ b/solution.py
@@ -18,12 +18,11 @@
 L = 128
 PAD = 32
 OWN_SUB = 768
-RIM_SUB = 256
 QUADS = 7
 CHUNK = 256
 STEP = 384
 SEND_STEP = 192
-EARLY = 2
+EARLY = 1
 PEERS_AT_ONCE = 8
 MIB = 2**20
 MESH = pl.DeviceIdType.MESH
@@ -333,16 +332,12 @@
 
     to_upper.wait()
     to_lower.wait()
-    lower = jnp.where(me > 0, hrecv[0], jnp.zeros((), BF))
-    upper = jnp.where(me < N_SPACE - 1, hrecv[1], jnp.zeros((), BF))
-    rim[:, :L] = lower[:RIM_SUB]
-    rim[:HALO - RIM_SUB, L:2 * L] = lower[RIM_SUB:]
-    rim[HALO - RIM_SUB:, L:2 * L] = upper[:2 * RIM_SUB - HALO]
-    rim[:, 2 * L:] = upper[2 * RIM_SUB - HALO:]
+    rim[:, :L] = jnp.where(me > 0, hrecv[0], jnp.zeros((), BF))
+    rim[:, L:] = jnp.where(me < N_SPACE - 1, hrecv[1], jnp.zeros((), BF))
 
     iota_r = lane_iota(SEND_STEP)
     peers = SEND_STEP // CAP
-    rim_tiles = RIM_SUB // L
+    rim_tiles = HALO // L
 
     @pl.loop(0, VOX // SEND_STEP)
     def _(i):
@@ -350,7 +345,7 @@
         here = aligned(turn, SEND_STEP)
         which = which_buf[here, :]
         beyond = which - VOX // L
-        kind = jnp.floor(beyond * (1.0 / rim_tiles))
+        kind = jnp.floor((beyond + 0.5) * (1.0 / rim_tiles))
         top, low = (beyond - rim_tiles * kind).astype(BF), which.astype(BF)
         for k in range(OFFSETS):
             lanes = slice(k * L, (k + 1) * L)
@@ -358,7 +353,7 @@
             every = dot(hot, rim[...])
             kinds = jnp.broadcast_to(kind[:, k:k + 1], (SEND_STEP, L))
             picked = gath[here, lanes].astype(F32)
-            for j in range(3):
+            for j in range(2):
                 picked = jnp.where(kinds == j, every[:, j * L:(j + 1) * L], picked)
             gath[here, lanes] = picked.astype(BF)
         pre = pre_buf[here, :] + dot(gath[here, :OFFSETS * L], wpad[...])
@@ -410,8 +405,6 @@
             down.mine[(3 * quad + i) * C2:(3 * quad + i + 1) * C2] = packed
     down.mine[DOWN_TILES * C2:] = jnp.zeros((32 * DOWN_SHARE - DOWN_TILES * C2, L), F32)
     down.start_pair()
-    subm.start_column()
-    down.start_plane()
 
     def coarse_block(block):
         hits = onehot_of_row(cell - block * CHUNK, CHUNK)
@@ -419,12 +412,14 @@
         coarse_ref[0, :, block * CHUNK:(block + 1) * CHUNK] = dot(cells, wdpad[...]).T[:C2].astype(BF)
 
     coarse_block(0)
+    subm.start_column()
+    down.start_plane()
+    coarse_block(1)
     subm.start_back()
     down.start_column()
-    coarse_block(1)
+    coarse_block(2)
     subm.start_over()
     down.start_back()
-    coarse_block(2)
     down.start_over()
     subm.finish()
 
@@ -469,7 +464,7 @@
             pltpu.VMEM((VOX, 2 * L), BF),
             pltpu.VMEM((VOX, L), BF),
             pltpu.VMEM((OWN_SUB, 2 * L), BF),
-            pltpu.VMEM((RIM_SUB, 3 * L), BF),
+            pltpu.VMEM((HALO, 2 * L), BF),
             pltpu.VMEM((VOX, L), F32),
             pltpu.VMEM((OFFSETS * L, L), BF),
             pltpu.VMEM((CHILDREN * L, 2 * L), BF),

time: 88.9 us -> 88.2 us (level)
  no operation moved by 1% of the time
where the time goes in v1:
time: 88.2 us; the launch traced here: 88.1 us
  Pallas kernels  87.5 us (99%)
    pallas_call x1, Pallas kernels, per_device(): pl.pallas_call(step_kernel, out_shape=(jax.ShapeDtypeStruct((1, C2, COARS...  84.1 us
    pallas_call x1, Pallas kernels, per_device(): pl.pallas_call(unpack_kernel, out_shape=(jax.ShapeDtypeStruct((1, C2, COA...  3.36 us

profile of v1, /device:TPU:1, one launch (start us, length us, event | category | flops | bytes accessed | tf_op | source)
XLA Modules:
  0.0 88.1 jit_solution(10696472683833162742)
XLA Ops:
  0.6 84.1 %step.1 = (bf16[1,192,768]{2,1,0:T(8,128)(2,1)}, bf16[2048,128]{1,0:T(8,128)(2,1)}, bf16[1536,128]{1,0:T(8,128)(2,1)}) custom-call(bf16[1,96,1536]{2,1,0:T(8,128)(2,1)} %feats_ref.1, s32[27,1,1536]{2,1,0:T(1,128)} %bitcast.1, s32[1,384]{1,0:T(1,128)} %up_ref.1, s32[1,384]{1,0:T(1,128)} %down_ref.1, s32[1,1536]{1,0:T(1,128)} %route_ref.1, ...), custom_call_target="tpu_custom_call" | custom-call | tf_op jit(solution)/shard_map/step/pallas_call | solution.py:454
  84.7 3.4 %unpack.1 = (bf16[1,192,768]{2,1,0:T(8,128)(2,1)}, f32[27,96,96]{2,1,0:T(8,128)}, f32[8,96,192]{2,1,0:T(8,128)}) custom-call(bf16[1,192,768]{2,1,0:T(8,128)(2,1)} %get-tuple-element.6.coarse_in, bf16[2048,128]{1,0:T(8,128)(2,1)} %get-tuple-element.7.subm_ref, bf16[1536,128]{1,0:T(8,128)(2,1)} %get-tuple-element.8.down_ref), custom_call_target="tpu_custom_call" | custom-call | tf_op jit(solution)/shard_map/unpack/pallas_call | solution.py:493

commit v2 on v1

--- a/solution.py
+++ b/solution.py
@@ -21,7 +21,7 @@
 QUADS = 7
 CHUNK = 256
 STEP = 384
-SEND_STEP = 192
+SEND_STEP = 384
 EARLY = 1
 PEERS_AT_ONCE = 8
 MIB = 2**20

time: 88.2 us -> 90.2 us (1.023)
  Pallas kernels: 87.5 us -> 89.4 us
    pallas_call x1, Pallas kernels: 84.1 us -> 86 us  [per_device(): pl.pallas_call(step_kernel, out_shape=(jax.ShapeDtypeStruct((1, C2, COARS...]
where the time goes in v2:
time: 90.2 us; the launch traced here: 90 us
  Pallas kernels  89.4 us (99%)
    pallas_call x1, Pallas kernels, per_device(): pl.pallas_call(step_kernel, out_shape=(jax.ShapeDtypeStruct((1, C2, COARS...  86 us
    pallas_call x1, Pallas kernels, per_device(): pl.pallas_call(unpack_kernel, out_shape=(jax.ShapeDtypeStruct((1, C2, COA...  3.36 us

profile of v2, /device:TPU:1, one launch (start us, length us, event | category | flops | bytes accessed | tf_op | source)
XLA Modules:
  0.0 90.0 jit_solution(6987420321922775245)
XLA Ops:
  0.6 86.0 %step.1 = (bf16[1,192,768]{2,1,0:T(8,128)(2,1)}, bf16[2048,128]{1,0:T(8,128)(2,1)}, bf16[1536,128]{1,0:T(8,128)(2,1)}) custom-call(bf16[1,96,1536]{2,1,0:T(8,128)(2,1)} %feats_ref.1, s32[27,1,1536]{2,1,0:T(1,128)} %bitcast.1, s32[1,384]{1,0:T(1,128)} %up_ref.1, s32[1,384]{1,0:T(1,128)} %down_ref.1, s32[1,1536]{1,0:T(1,128)} %route_ref.1, ...), custom_call_target="tpu_custom_call" | custom-call | tf_op jit(solution)/shard_map/step/pallas_call | solution.py:454
  86.7 3.4 %unpack.1 = (bf16[1,192,768]{2,1,0:T(8,128)(2,1)}, f32[27,96,96]{2,1,0:T(8,128)}, f32[8,96,192]{2,1,0:T(8,128)}) custom-call(bf16[1,192,768]{2,1,0:T(8,128)(2,1)} %get-tuple-element.6.coarse_in, bf16[2048,128]{1,0:T(8,128)(2,1)} %get-tuple-element.7.subm_ref, bf16[1536,128]{1,0:T(8,128)(2,1)} %get-tuple-element.8.down_ref), custom_call_target="tpu_custom_call" | custom-call | tf_op jit(solution)/shard_map/unpack/pallas_call | solution.py:493
